TPU v7x, 32 devices: a whole 2x2x4 slice. The times are simulated.
32 devices in a mesh: store: 8 (over z, x), tensor: 4 (over y, core).
Axes of the slice: x: 2, y: 2, z: 4, core: 2. Of those that a mesh axis runs over, the one named last changes fastest.
Arguments:
- hidden: bfloat16 [8192, 12288], P('store', 'tensor'), may hold values from -6 to 6
- kv_weight: bfloat16 [12288, 2048], P('tensor', 'store'), may hold values from -0.0546875 to 0.0546875
- pages: bfloat16 [256, 128, 2048], P('store', None, 'tensor'), may hold values from -8 to 8
- queries: bfloat16 [8192, 6144], P('store', 'tensor'), may hold values from -8 to 8
- page_owner: int32 [16, 16], replicated, may hold values from 0 to 7, as said below
- page_slot: int32 [16, 16], replicated, may hold values from 0 to 31
- span_order: int32 [16, 16], P('store'), may hold values from 0 to 15, each once within a row
- positions: int32 [16, 16, 32], P('store'), may hold values from 2 to 127, as said below
- counts: int32 [16, 16], P('store'), may hold values from 1 to 32, as said below
Outputs:
- attended: bfloat16 [8192, 6144], P('store', 'tensor')
- new_kv: bfloat16 [8192, 2048], P('store', 'tensor')
Inputs may be any that keep to these rules, and one draw needn't show every extreme that they name: `page_owner`: request r is served at store index r // 2. Among the 32 pages of the requests served at one store index, each owner holds at most 8, and some owner exactly 8. `positions`: each row increases strictly. `counts`: every request has a span with 32.
All inputs are finite; a program needn't handle non-finite values.
Results may differ from a plain program's by a relative error of at most 0.0053.
Values may be sent and summed in bfloat16 or wider, within the bound.
A program may use at most 128 MiB of HBM per device.

v0:
```python
import jax
import jax.numpy as jnp
from jax import lax
from jax.sharding import PartitionSpec as P

HEAD = 128


def blend_attend(request_queries, fresh_rows, cached, span_rank, recompute_pos, row_used):
    spans, span_len, kv_width = cached.shape
    per_span = recompute_pos.shape[1]
    kv_heads = kv_width // (2 * HEAD)
    head_group = request_queries.shape[1] // (kv_heads * HEAD)
    marked = (recompute_pos[:, :, None] == jnp.arange(span_len)[None, None, :]) & row_used[
        :, :, None
    ]
    placed = jnp.einsum(
        "cjt,cjw->ctw",
        marked.astype(jnp.bfloat16),
        fresh_rows.reshape(spans, per_span, kv_width),
        preferred_element_type=jnp.float32,
    )
    replaced = jnp.any(marked, axis=1)[:, :, None]
    blended = jnp.where(replaced, placed.astype(jnp.bfloat16), cached)
    key_value = blended.reshape(spans * span_len, kv_heads, 2, HEAD)
    query_rows = request_queries.reshape(spans * per_span, kv_heads, head_group, HEAD)
    scores = jnp.einsum(
        "qhgd,khd->hgqk", query_rows, key_value[:, :, 0], preferred_element_type=jnp.float32
    ) * HEAD ** (-0.5)
    query_span = jnp.arange(spans * per_span) // per_span
    key_span = jnp.arange(spans * span_len) // span_len
    key_place = jnp.arange(spans * span_len) % span_len
    query_place = recompute_pos.reshape(-1)
    query_rank = jnp.repeat(span_rank, per_span)
    key_rank = jnp.repeat(span_rank, span_len)
    earlier = key_rank[None, :] < query_rank[:, None]
    causal = (key_span[None, :] == query_span[:, None]) & (
        key_place[None, :] <= query_place[:, None]
    )
    allowed = earlier | causal
    scores = jnp.where(allowed[None, None], scores, -1e30)
    peak = jnp.max(scores, axis=-1, keepdims=True)
    raised = jnp.exp(scores - peak)
    weights = (raised / jnp.sum(raised, axis=-1, keepdims=True)).astype(jnp.bfloat16)
    mixed = jnp.einsum(
        "hgqk,khd->qhgd", weights, key_value[:, :, 1], preferred_element_type=jnp.float32
    )
    mixed = mixed.reshape(spans * per_span, -1) * row_used.reshape(-1, 1).astype(jnp.float32)
    return mixed.astype(jnp.bfloat16)


def body(hidden, kv_weight, pages, queries, page_owner, page_slot, span_order, positions, counts):
    store_count = lax.axis_size("store")
    store_index = lax.axis_index("store")
    req_local, spans = span_order.shape
    per_span = positions.shape[2]
    entries = req_local * spans
    slot_depth = max(2, 2 * entries // store_count)
    span_len = pages.shape[1]
    kv_width = pages.shape[2]
    partial_kv = jnp.dot(
        hidden,
        lax.all_gather(kv_weight, "store", axis=1, tiled=True),
        preferred_element_type=jnp.float32,
    )
    summed = lax.psum(partial_kv, "tensor")
    own_kv = lax.dynamic_slice_in_dim(summed, lax.axis_index("tensor") * kv_width, kv_width, 1)
    row_used = jnp.arange(per_span)[None, None, :] < counts[:, :, None]
    new_kv = (own_kv * row_used.reshape(-1, 1).astype(jnp.float32)).astype(jnp.bfloat16)
    owners = page_owner.reshape(store_count, entries)
    slot_table = page_slot.reshape(store_count, entries)
    before = jnp.arange(entries)[None, :] < jnp.arange(entries)[:, None]
    same_owner = owners[:, :, None] == owners[:, None, :]
    owner_rank = jnp.sum(same_owner & before[None], axis=2)
    picked = (owners == store_index)[:, :, None] & (
        owner_rank[:, :, None] == jnp.arange(slot_depth)[None, None, :]
    )
    source_slot = jnp.sum(picked * slot_table[:, :, None], axis=1)
    filled = jnp.any(picked, axis=1)
    outgoing = jnp.take(pages, source_slot.reshape(-1), axis=0)
    outgoing = jnp.where(filled.reshape(-1, 1, 1), outgoing, jnp.zeros((), jnp.bfloat16))
    outgoing = outgoing.reshape(store_count, slot_depth, span_len, kv_width)
    arrived = lax.all_to_all(outgoing, "store", split_axis=0, concat_axis=0, tiled=True)
    my_owner = lax.dynamic_index_in_dim(owners, store_index, 0, keepdims=False)
    my_rank = lax.dynamic_index_in_dim(owner_rank, store_index, 0, keepdims=False)
    flat_index = my_owner * slot_depth + my_rank
    cached = jnp.take(
        arrived.reshape(store_count * slot_depth, span_len, kv_width), flat_index, axis=0
    )
    cached = cached.reshape(req_local, spans, span_len, kv_width)
    query_request = queries.reshape(req_local, spans * per_span, queries.shape[1])
    fresh_request = new_kv.reshape(req_local, spans * per_span, kv_width)

    def one_request(inputs):
        return blend_attend(*inputs)

    attended = lax.map(
        one_request, (query_request, fresh_request, cached, span_order, positions, row_used)
    )
    return (attended.reshape(queries.shape), new_kv)


def solution(mesh):
    placed = (
        P("store", "tensor"),
        P("tensor", "store"),
        P("store", None, "tensor"),
        P("store", "tensor"),
        P(),
        P(),
        P("store", None),
        P("store", None, None),
        P("store", None),
    )
    return jax.shard_map(
        body,
        mesh=mesh,
        in_specs=placed,
        out_specs=(P("store", "tensor"), P("store", "tensor")),
        check_vma=False,
    )
```

profile of v0, /device:TPU:0, one launch (start us, length us, event | category | flops | bytes accessed | tf_op | source)
XLA Modules:
  0.0 680.7 jit_solution(10282494463625117020)
XLA Ops:
  7.2 0.0 all-gather.2.cloned.1.call-start
  7.2 0.7 all-gather.2.cloned.1.call-update
  7.9 0.8 reshape.382
  8.7 0.8 mul.73
  9.4 0.3 convert_reduce_fusion
  9.8 0.2 select_reduce_fusion
  10.0 0.1 reshape.383
  10.1 7.6 %gather_fusion = bf16[64,128,512]{2,1,0:T(8,128)(2,1)} fusion(bf16[32,128,512]{2,1,0:T(8,128)(2,1)} %param.13, s32[1024]{0:T(1024)S(1)} %pad_clamp_fusion.1), kind=kCustom, calls=%fused_computation | custom fusion | bytes 16777472 | tf_op jit(solution)/shard_map/jit(_take)/gather | solution.py:80
  17.7 0.2 fusion.29
  17.9 8.5 %select_select_fusion = bf16[8,8,128,512]{3,2,1,0:T(8,128)(2,1)} fusion(bf16[8,8,128,512]{3,2,1,0:T(8,128)(2,1)} %bitcast.91, pred[8,8]{1,0:T(8,128)(4,1)S(1)} %compare_and_fusion, pred[8,8]{1,0:T(8,128)(4,1)S(1)} %fusion.29), kind=kLoop, calls=%fused_computation.52 | loop fusion | flops 8388608 | bytes 16777344 | tf_op jit(solution)/shard_map/jit(_where)/select_n | solution.py:81
  26.5 7.4 %all-to-all-start = ((bf16[8,8,128,512]{3,2,1,0:T(8,128)(2,1)}), bf16[8,8,128,512]{3,2,1,0:T(8,128)(2,1)}, u32[]{:S(2)}, u32[]{:S(2)}) async-start(bf16[8,8,128,512]{3,2,1,0:T(8,128)(2,1)} %select_select_fusion), calls=%async_computation | async-start | bytes 16777216 | tf_op jit(solution)/shard_map/all_to_all | solution.py:83
  33.8 0.0 all-reduce.2.cloned.1.call-start
  33.9 326.6 %all-gather.2.cloned.1.call-done = bf16[3072,2048]{1,0:T(8,128)(2,1)} async-done(((bf16[3072,256]{1,0:T(8,128)(2,1)}), bf16[3072,2048]{1,0:T(8,128)(2,1)}) %all-gather.2.cloned.1.call-update) | async-done | bytes 12582928 | tf_op jit(solution)/shard_map/all_gather | solution.py:63
  360.5 18.8 %fusion.39 = f32[1024,2048]{1,0:T(8,128)} fusion(bf16[1024,3072]{1,0:T(8,128)(2,1)} %param.11, bf16[3072,2048]{1,0:T(8,128)(2,1)} %all-gather.2.cloned.1.call-done), kind=kOutput, calls=%fused_computation.81 | convolution fusion | flops 12884901888 | bytes 27262976 | tf_op jit(solution)/shard_map/dot_general | solution.py:61
  379.2 0.0 all-reduce.2.cloned.1.call-update
  379.3 0.5 broadcast.357
  379.8 0.7 fusion.35
  380.4 0.1 add.115
  380.5 0.1 fusion.34
  380.6 0.1 reshape.388
  380.7 0.0 all-to-all-done
  380.7 7.0 %gather_fusion.1 = bf16[32,128,512]{2,1,0:T(8,128)(2,1)} fusion(bf16[64,128,512]{2,1,0:T(8,128)(2,1)} %bitcast.19, s32[1024]{0:T(1024)S(1)} %pad_clamp_fusion), kind=kCustom, calls=%fused_computation.1 | custom fusion | bytes 8388736 | tf_op jit(solution)/shard_map/jit(_take)/gather | solution.py:87
  387.7 4.8 broadcast_select_fusion
  392.5 136.9 %all-reduce.2.cloned.1.call-done = f32[1024,2048]{1,0:T(8,128)} async-done(((f32[1024,2048]{1,0:T(8,128)}), f32[1024,2048]{1,0:T(8,128)}) %all-reduce.2.cloned.1.call-update) | async-done | bytes 8388624 | tf_op jit(solution)/shard_map/psum | solution.py:66
  529.4 2.8 multiply_convert_fusion.1
  532.2 141.6 %while.13 = (s32[]{:T(128)}, bf16[2,512,1536]{2,1,0:T(8,128)(2,1)}, s32[2,16,32]{2,1,0:T(8,128)S(1)}, pred[2,16,32]{2,1,0:T(8,128)(4,1)S(1)}, bf16[2,512,512]{2,...) while((s32[]{:T(128)}, bf16[2,512,1536]{2,1,0:T(8,128)(2,1)}, ...), condition=%wide.region_8.9_spmd, body=%wide.region_4.8_spmd.sunk | while | flops 6594327040 | bytes 143274384 | solution.py:97
  532.2 0.1 broadcast_bitcast_fusion.2
  532.3 0.1 broadcast_in_dim.140
  532.4 0.1 lt.185
  532.4 0.1 le.65
  532.5 0.1 reshape.419
  532.6 0.2 fusion.64
  532.8 1.1 constant_dynamic-slice_fusion.11
  533.9 2.0 and_or_fusion.2
  535.9 4.0 bitcast_select_fusion.6
  539.9 2.5 reshape.418
  542.5 2.7 constant_dynamic-slice_fusion.10
  545.1 2.6 copy.57
  547.7 4.2 fusion.65
  551.9 4.6 copy.58
  556.4 27.3 %fusion.66 = (f32[2,6,512]{2,1,0:T(8,128)S(1)}, f32[2,6,512,2048]{2,3,1,0:T(8,128)}) fusion(pred[512,2048]{0,1:T(8,128)(4,1)S(1)} %and_or_fusion.2, bf16[512,2,6,128]{0,3,2,1:T(8,128)(2,1)} %bitcast.90, bf16[2048,2,1,128]{3,2,1,0:T(2,128)(2,1)} %get-tuple-element.242), kind=kOutput, calls=%fused_computation.80.clone.1 | convolution fusion | flops 3271559168 | bytes 54026240 | tf_op jit(solution)/shard_map/while/body/eval_jaxpr/sub | solution.py:43
  583.7 16.9 %fusion.67 = f32[2,128,6,512]{3,1,2,0:T(8,128)S(1)} fusion(f32[2,6,512,2048]{2,3,1,0:T(8,128)} %get-tuple-element.243, f32[2,6,512]{2,1,0:T(8,128)S(1)} %get-tuple-element.244, bf16[2048,2,1,128]{0,3,1,2:T(8,128)(2,1)S(1)} %copy.58), kind=kOutput, calls=%fused_computation.10.clone.1 | convolution fusion | flops 3246391296 | bytes 54550528 | tf_op jit(solution)/shard_map/while/body/eval_jaxpr/hgqk,khd->qhgd/dot_general | solution.py:45
  600.6 0.5 multiply_convert_fusion.3
  601.0 0.7 copy.59
  601.8 1.2 constant_dynamic-update-slice_fusion.2
  603.0 0.1 broadcast_bitcast_fusion.2
  603.1 0.1 broadcast_in_dim.140
  603.2 0.1 lt.185
  603.3 0.1 le.65
  603.3 0.1 reshape.419
  603.4 0.2 fusion.64
  603.7 1.1 constant_dynamic-slice_fusion.11
  604.7 2.0 and_or_fusion.2
  606.7 4.0 bitcast_select_fusion.6
  610.7 2.5 reshape.418
  613.3 2.7 constant_dynamic-slice_fusion.10
  615.9 2.6 copy.57
  618.5 4.2 fusion.65
  622.7 4.6 copy.58
  627.2 27.3 %fusion.66 = (f32[2,6,512]{2,1,0:T(8,128)S(1)}, f32[2,6,512,2048]{2,3,1,0:T(8,128)}) fusion(pred[512,2048]{0,1:T(8,128)(4,1)S(1)} %and_or_fusion.2, bf16[512,2,6,128]{0,3,2,1:T(8,128)(2,1)} %bitcast.90, bf16[2048,2,1,128]{3,2,1,0:T(2,128)(2,1)} %get-tuple-element.242), kind=kOutput, calls=%fused_computation.80.clone.1 | convolution fusion | flops 3271559168 | bytes 54026240 | tf_op jit(solution)/shard_map/while/body/eval_jaxpr/sub | solution.py:43
  654.5 16.9 %fusion.67 = f32[2,128,6,512]{3,1,2,0:T(8,128)S(1)} fusion(f32[2,6,512,2048]{2,3,1,0:T(8,128)} %get-tuple-element.243, f32[2,6,512]{2,1,0:T(8,128)S(1)} %get-tuple-element.244, bf16[2048,2,1,128]{0,3,1,2:T(8,128)(2,1)S(1)} %copy.58), kind=kOutput, calls=%fused_computation.10.clone.1 | convolution fusion | flops 3246391296 | bytes 54550528 | tf_op jit(solution)/shard_map/while/body/eval_jaxpr/hgqk,khd->qhgd/dot_general | solution.py:45
  671.4 0.5 multiply_convert_fusion.3
  671.9 0.7 copy.59
  672.6 1.2 constant_dynamic-update-slice_fusion.2
  (27 shorter events, 0.1 us)
Async XLA Ops:
  7.2 353.3 %all-gather.2.cloned.1.call-start = ((), (), s32[]{:S(2)}) async-start(), calls=%async_computation.1 | async-start | bytes 14155776 | tf_op jit(solution)/shard_map/all_gather | solution.py:63
  26.5 354.2 %all-to-all-start = ((bf16[8,8,128,512]{3,2,1,0:T(8,128)(2,1)}), bf16[8,8,128,512]{3,2,1,0:T(8,128)(2,1)}, u32[]{:S(2)}, u32[]{:S(2)}) async-start(bf16[8,8,128,512]{3,2,1,0:T(8,128)(2,1)} %select_select_fusion), calls=%async_computation | async-start | bytes 16777216 | tf_op jit(solution)/shard_map/all_to_all | solution.py:83
  33.8 495.6 %all-reduce.2.cloned.1.call-start = ((), (), s32[]{:S(2)}) async-start(), calls=%async_computation.2 | async-start | bytes 16777216 | tf_op jit(solution)/shard_map/psum | solution.py:66
  379.2 1.3 copy-start.1
  387.7 144.5 %copy-start = (s32[2,16,32]{2,1,0:T(8,128)S(1)}, s32[2,16,32]{2,1,0:T(8,128)}, u32[]{:S(2)}) copy-start(s32[2,16,32]{2,1,0:T(8,128)} %param.18) | copy-start | bytes 12292
  387.7 144.5 %copy-start.2 = (s32[2,16]{1,0:T(2,128)S(1)}, s32[2,16]{1,0:T(2,128)}, u32[]{:S(2)}) copy-start(s32[2,16]{1,0:T(2,128)} %param.17) | copy-start | bytes 388
Sparse Core Ops, SparseCore 0:
  10.0 350.3 all-gather.1
  379.4 149.9 all-reduce.1
where the time goes:
time: 682 us; the launch traced here: 681 us
  waiting for transfers between devices  464 us (68%)
  matrix products  115 us (17%)
  local copies, waits for them, and re-layouts  56.7 us (8%)
  other arithmetic  23 us (3%)
  between operations  14.1 us (2%)
  starting transfers between devices  7.45 us (1%)
    all_gather x1, waiting for transfers between devices, body(): lax.all_gather(kv_weight, 'store', axis=1, tiled=True)  327 us
    psum x1, waiting for transfers between devices, body(): summed = lax.psum(partial_kv, 'tensor')  137 us
    sub x2, matrix products, blend_attend(): raised = jnp.exp(scores - peak)  54.6 us
    dot_general x2, matrix products, blend_attend(): jnp.einsum('hgqk,khd->qhgd', weights, key_value[:, :, 1], preferred_eleme...  33.7 us
    dot_general x1, matrix products, body(): jnp.dot(hidden, lax.all_gather(kv_weight, 'store', axis=1, tiled=True), p...  18.8 us
  transfers between devices with their start and end apart: 3, of which 2 were waited for; matrix products, arithmetic and copies ran while one was open for 7% of the time, Pallas kernels for 0%

commit v1 on v0

v1 whole, which is shorter than its diff:
```python
import functools

import jax
import jax.numpy as jnp
from jax import lax
from jax.experimental import pallas as pl
from jax.experimental.pallas import tpu as pltpu
from jax.sharding import PartitionSpec as P

HEAD = 128
MESH_ID = pl.DeviceIdType.MESH
ROW_TILE = 256
VMEM_BYTES = 60 * 1024 * 1024


def exchange_kernel(
    line, tensors, hid_ref, w_ref, out_ref, used_ref, kv_ref, arr_ref,
    wbuf, own, sendbuf, recvbuf,
    loc_sem, up_sem, dn_sem, x_sem, wrecv, psend, precv, rsend, rrecv,
):
    me = lax.axis_index("store")
    tm = lax.axis_index("tensor")
    n = 2 * line
    a, b = me // 2, me % 2
    width = w_ref.shape[1]
    per_owner = (n * width) // (tensors * width)

    barrier = pltpu.get_barrier_semaphore()
    for j in range(1, n):
        pl.semaphore_signal(
            barrier, inc=1, device_id=((me + j) % n, tm), device_id_type=MESH_ID
        )
    for j in range(1, tensors):
        pl.semaphore_signal(
            barrier, inc=1, device_id=(me, (tm + j) % tensors), device_id_type=MESH_ID
        )
    own_w = pltpu.make_async_copy(w_ref, wbuf.at[me], loc_sem.at[0])
    own_w.start()
    own_pages = pltpu.make_async_copy(out_ref.at[me], arr_ref.at[me], loc_sem.at[1])
    own_pages.start()
    own_w.wait()
    pl.semaphore_wait(barrier, n - 1 + tensors - 1)

    def w_copy(slot, sem, dest):
        return pltpu.make_async_remote_copy(
            src_ref=wbuf.at[slot], dst_ref=wbuf.at[slot], send_sem=sem.at[slot],
            recv_sem=wrecv.at[slot], device_id=(dest, tm), device_id_type=MESH_ID,
        )

    def up(slot):
        return w_copy(slot, up_sem, jnp.minimum(me + 2, n - 2 + b))

    def down(slot):
        return w_copy(slot, dn_sem, jnp.maximum(me - 2, b))

    def across(slot):
        return w_copy(slot, x_sem, a * 2 + 1 - b)

    def got(slot):
        across(slot).wait_recv()

    def page_copy(dest):
        return pltpu.make_async_remote_copy(
            src_ref=out_ref.at[dest], dst_ref=arr_ref.at[me], send_sem=psend.at[dest],
            recv_sem=precv.at[me], device_id=(dest, tm), device_id_type=MESH_ID,
        )

    def page_wait(src):
        pltpu.make_async_remote_copy(
            src_ref=out_ref.at[src], dst_ref=arr_ref.at[src], send_sem=psend.at[src],
            recv_sem=precv.at[src], device_id=(src, tm), device_id_type=MESH_ID,
        ).wait_recv()

    def part_copy(slot):
        return pltpu.make_async_remote_copy(
            src_ref=sendbuf.at[slot], dst_ref=recvbuf.at[tm, slot % per_owner],
            send_sem=rsend.at[slot], recv_sem=rrecv.at[tm, slot % per_owner],
            device_id=(me, slot // per_owner), device_id_type=MESH_ID,
        )

    def compute(slot):
        mine = slot // per_owner == tm

        def tile(i, carry):
            rows = pl.ds(pl.multiple_of(i * ROW_TILE, ROW_TILE), ROW_TILE)
            part = jnp.dot(hid_ref[rows, :], wbuf[slot], preferred_element_type=jnp.float32)

            @pl.when(mine)
            def _():
                own[slot % per_owner, rows, :] = part

            @pl.when(jnp.logical_not(mine))
            def _():
                sendbuf[slot, rows, :] = part.astype(sendbuf.dtype)

            return carry

        lax.fori_loop(0, hid_ref.shape[0] // ROW_TILE, tile, 0)

        @pl.when(jnp.logical_not(mine))
        def _():
            part_copy(slot).start()

    @pl.when(a < line - 1)
    def _():
        up(me).start()

    @pl.when(a > 0)
    def _():
        down(me).start()

    across(me).start()
    compute(me)

    def hop(k, carry):
        low, high = a - k, a + k

        @pl.when(low >= 0)
        def _():
            slot = low * 2 + b
            got(slot)

            @pl.when(a < line - 1)
            def _():
                up(slot).start()

            across(slot).start()

        @pl.when(high < line)
        def _():
            slot = high * 2 + b
            got(slot)

            @pl.when(a > 0)
            def _():
                down(slot).start()

            across(slot).start()

        @pl.when(k == 1)
        def _():
            def same(i, c):
                page_copy(((a + i) % line) * 2 + b).start()
                return c

            lax.fori_loop(1, line, same, 0)

        @pl.when(k == line - 1)
        def _():
            def other(i, c):
                page_copy(((a + i) % line) * 2 + 1 - b).start()
                return c

            lax.fori_loop(0, line, other, 0)

        for place in (low, high):
            @pl.when((place >= 0) & (place < line))
            def _(place=place):
                compute(place * 2 + b)

        return carry

    lax.fori_loop(1, line, hop, 0)

    def cross(k, carry):
        for place in (a - k, a + k):
            @pl.when((place >= 0) & (place < line))
            def _(place=place):
                slot = place * 2 + 1 - b
                got(slot)
                compute(slot)

        return carry

    slot0 = a * 2 + 1 - b
    got(slot0)
    compute(slot0)
    lax.fori_loop(1, line, cross, 0)

    def collect(j, carry):
        src = (tm + j) % tensors
        for q in range(per_owner):
            pltpu.make_async_remote_copy(
                src_ref=sendbuf.at[q], dst_ref=recvbuf.at[src, q], send_sem=rsend.at[q],
                recv_sem=rrecv.at[src, q], device_id=(me, src), device_id_type=MESH_ID,
            ).wait_recv()
        return carry

    lax.fori_loop(1, tensors, collect, 0)

    def finish(i, carry):
        rows = pl.ds(pl.multiple_of(i * ROW_TILE, ROW_TILE), ROW_TILE)
        for q in range(per_owner):
            total = own[q, rows, :]
            for j in range(1, tensors):
                total += recvbuf[(tm + j) % tensors, q, rows, :].astype(jnp.float32)
            kv_ref[rows, q * width : (q + 1) * width] = (total * used_ref[rows, :]).astype(
                kv_ref.dtype
            )
        return carry

    lax.fori_loop(0, hid_ref.shape[0] // ROW_TILE, finish, 0)

    def drain(slot, carry):
        @pl.when(slot // per_owner != tm)
        def _():
            part_copy(slot).wait_send()

        @pl.when(slot % 2 == b)
        def _():
            across(slot).wait_send()

            @pl.when((slot // 2 <= a) & (a < line - 1))
            def _():
                up(slot).wait_send()

            @pl.when((slot // 2 >= a) & (a > 0))
            def _():
                down(slot).wait_send()

        @pl.when(slot != me)
        def _():
            page_copy(slot).wait_send()
            page_wait(slot)

        return carry

    lax.fori_loop(0, n, drain, 0)
    own_pages.wait()


def exchange(hidden, kv_weight, outgoing, used, n, tensors):
    rows, depth = hidden.shape
    width = kv_weight.shape[1]
    per_owner = n // tensors
    dma = pltpu.SemaphoreType.DMA
    return pl.pallas_call(
        functools.partial(exchange_kernel, n // 2, tensors),
        out_shape=(
            jax.ShapeDtypeStruct((rows, per_owner * width), jnp.bfloat16),
            jax.ShapeDtypeStruct(outgoing.shape, outgoing.dtype),
        ),
        in_specs=[
            pl.BlockSpec(memory_space=pltpu.VMEM),
            pl.BlockSpec(memory_space=pl.ANY),
            pl.BlockSpec(memory_space=pl.ANY),
            pl.BlockSpec(memory_space=pltpu.VMEM),
        ],
        out_specs=(
            pl.BlockSpec(memory_space=pltpu.VMEM),
            pl.BlockSpec(memory_space=pl.ANY),
        ),
        scratch_shapes=[
            pltpu.VMEM((n, depth, width), jnp.bfloat16),
            pltpu.VMEM((per_owner, rows, width), jnp.float32),
            pltpu.VMEM((n, rows, width), jnp.bfloat16),
            pltpu.VMEM((tensors, per_owner, rows, width), jnp.bfloat16),
            dma((2,)), dma((n,)), dma((n,)), dma((n,)), dma((n,)),
            dma((n,)), dma((n,)), dma((n,)), dma((tensors, per_owner)),
        ],
        compiler_params=pltpu.CompilerParams(
            collective_id=0, has_side_effects=True, vmem_limit_bytes=VMEM_BYTES
        ),
        cost_estimate=pl.CostEstimate(
            flops=2 * rows * depth * n * width, bytes_accessed=4 * 10**7, transcendentals=0
        ),
    )(hidden, kv_weight, outgoing, used)


GROUP = 4


def attend_kernel(
    reqs, spans, per_span, span_len, heads, fold,
    page_sref, span_sref, q_ref, kv_ref, pos_col, used_col, pos_row, arr_ref, out_ref,
    page, keys, qbuf, sbuf, lim, page_sem,
):
    def fetch(i):
        return pltpu.make_async_copy(arr_ref.at[page_sref[i]], page.at[i], page_sem.at[i])

    def start(i, c):
        fetch(i).start()
        return c

    lax.fori_loop(0, reqs * spans, start, 0)

    def blend(i, c):
        fetch(i).wait()
        span = span_sref[i]
        marks = pos_row[pl.ds(span, 1), :]
        hit = lax.broadcasted_iota(jnp.int32, (span_len, per_span), 0) == marks
        fresh = kv_ref[pl.ds(pl.multiple_of(span * per_span, per_span), per_span), :]
        placed = jnp.dot(
            hit.astype(jnp.float32).astype(jnp.bfloat16), fresh,
            preferred_element_type=jnp.float32,
        )
        replaced = jnp.max(hit.astype(jnp.float32), axis=1, keepdims=True) > 0.5
        mixed = jnp.where(replaced, placed, page[i].astype(jnp.float32))
        keys[pl.ds(pl.multiple_of(i * span_len, span_len), span_len), :] = mixed.astype(
            jnp.bfloat16
        )
        return c

    lax.fori_loop(0, reqs * spans, blend, 0)
    scale = HEAD ** (-0.5)
    block = fold * per_span

    def one(i, carry):
        r = i // (spans // GROUP)
        for g_static in range(spans // GROUP):
            @pl.when(i % (spans // GROUP) == g_static)
            def _(g=g_static):
                length = (g + 1) * GROUP * span_len
                free = g * GROUP * span_len
                base = pl.multiple_of(r * spans * span_len, span_len)
                for h in range(heads):
                    for ii in range(GROUP):
                        span = span_sref[r * spans + g * GROUP + ii]
                        rows = pl.ds(pl.multiple_of(span * per_span, per_span), per_span)
                        limit = pos_col[rows, :] + ii * span_len
                        for m in range(fold):
                            col = (h * fold + m) * HEAD
                            at = ii * block + m * per_span
                            qbuf[at : at + per_span, :] = q_ref[rows, col : col + HEAD]
                            if h == 0:
                                lim[at : at + per_span, :] = limit
                    key = keys[pl.ds(base, length), 2 * h * HEAD : (2 * h + 1) * HEAD]
                    val = keys[pl.ds(base, length), (2 * h + 1) * HEAD : (2 * h + 2) * HEAD]
                    sbuf[:, :length] = lax.dot_general(
                        qbuf[...], key, (((1,), (1,)), ((), ())),
                        preferred_element_type=jnp.float32,
                    )
                    for ii in range(GROUP):
                        sl = slice(ii * block, (ii + 1) * block)
                        tail = sbuf[sl, free:length]
                        place = lax.broadcasted_iota(jnp.int32, tail.shape, 1)
                        tail = jnp.where(place <= lim[sl, :], tail, -1e30)
                        if g:
                            score = jnp.concatenate([sbuf[sl, :free], tail], axis=1)
                        else:
                            score = tail
                        peak = jnp.max(score, axis=1, keepdims=True)
                        raised = jnp.exp((score - peak) * scale)
                        total = jnp.sum(raised, axis=1, keepdims=True)
                        mixed = jnp.dot(
                            raised.astype(jnp.bfloat16), val, preferred_element_type=jnp.float32
                        ) / total
                        span = span_sref[r * spans + g * GROUP + ii]
                        rows = pl.ds(pl.multiple_of(span * per_span, per_span), per_span)
                        used = used_col[rows, :]
                        for m in range(fold):
                            col = (h * fold + m) * HEAD
                            out_ref[rows, col : col + HEAD] = (
                                mixed[m * per_span : (m + 1) * per_span, :] * used
                            ).astype(out_ref.dtype)
        return carry

    lax.fori_loop(0, reqs * (spans // GROUP), one, 0)


def attend(page_at, span_at, queries, new_kv, pos_col, used_col, pos_row, arrived, shape):
    reqs, spans, per_span, span_len = shape
    heads = new_kv.shape[1] // (2 * HEAD)
    fold = queries.shape[1] // (heads * HEAD)
    vm = pl.BlockSpec(memory_space=pltpu.VMEM)
    sm = pl.BlockSpec(memory_space=pltpu.SMEM)
    total = reqs * spans
    return pl.pallas_call(
        functools.partial(attend_kernel, reqs, spans, per_span, span_len, heads, fold),
        out_shape=jax.ShapeDtypeStruct(queries.shape, queries.dtype),
        in_specs=[sm, sm, vm, vm, vm, vm, vm, pl.BlockSpec(memory_space=pl.ANY)],
        out_specs=vm,
        scratch_shapes=[
            pltpu.VMEM((total, span_len, new_kv.shape[1]), jnp.bfloat16),
            pltpu.VMEM((total * span_len, new_kv.shape[1]), jnp.bfloat16),
            pltpu.VMEM((GROUP * fold * per_span, HEAD), jnp.bfloat16),
            pltpu.VMEM((GROUP * fold * per_span, spans * span_len), jnp.float32),
            pltpu.VMEM((GROUP * fold * per_span, 1), jnp.int32),
            pltpu.SemaphoreType.DMA((total,)),
        ],
        compiler_params=pltpu.CompilerParams(vmem_limit_bytes=VMEM_BYTES),
    )(page_at, span_at, queries, new_kv, pos_col, used_col, pos_row, arrived)


def body(hidden, kv_weight, pages, queries, page_owner, page_slot, span_order, positions, counts):
    store_count = lax.axis_size("store")
    tensors = lax.axis_size("tensor")
    store_index = lax.axis_index("store")
    req_local, spans = span_order.shape
    per_span = positions.shape[2]
    entries = req_local * spans
    slot_depth = max(2, 2 * entries // store_count)
    span_len = pages.shape[1]
    kv_width = pages.shape[2]
    row_used = jnp.arange(per_span)[None, None, :] < counts[:, :, None]
    used_col = row_used.reshape(-1, 1).astype(jnp.float32)
    owners = page_owner.reshape(store_count, entries)
    slot_table = page_slot.reshape(store_count, entries)
    before = jnp.arange(entries)[None, :] < jnp.arange(entries)[:, None]
    same_owner = owners[:, :, None] == owners[:, None, :]
    owner_rank = jnp.sum(same_owner & before[None], axis=2)
    picked = (owners == store_index)[:, :, None] & (
        owner_rank[:, :, None] == jnp.arange(slot_depth)[None, None, :]
    )
    source_slot = jnp.sum(picked * slot_table[:, :, None], axis=1)
    outgoing = jnp.take(pages, source_slot.reshape(-1), axis=0, mode="clip")
    outgoing = outgoing.reshape(store_count, slot_depth, span_len, kv_width)
    if kv_weight.shape[1] % 128 == 0 and store_count % tensors == 0:
        new_kv, arrived = exchange(hidden, kv_weight, outgoing, used_col, store_count, tensors)
    else:
        partial_kv = jnp.dot(
            hidden,
            lax.all_gather(kv_weight, "store", axis=1, tiled=True),
            preferred_element_type=jnp.float32,
        )
        own_kv = lax.psum_scatter(partial_kv, "tensor", scatter_dimension=1, tiled=True)
        new_kv = (own_kv * used_col).astype(jnp.bfloat16)
        arrived = lax.all_to_all(outgoing, "store", split_axis=0, concat_axis=0, tiled=True)
    my_owner = lax.dynamic_index_in_dim(owners, store_index, 0, keepdims=False)
    my_rank = lax.dynamic_index_in_dim(owner_rank, store_index, 0, keepdims=False)
    flat_index = (my_owner * slot_depth + my_rank).reshape(req_local, spans)
    is_place = span_order[:, None, :] == jnp.arange(spans)[None, :, None]
    span_at = jnp.sum(is_place * jnp.arange(spans)[None, None, :], axis=2)
    page_at = jnp.sum(is_place * flat_index[:, None, :], axis=2)
    span_at = (span_at + jnp.arange(req_local)[:, None] * spans).reshape(-1)
    attended = attend(
        page_at.reshape(-1).astype(jnp.int32), span_at.astype(jnp.int32), queries, new_kv,
        positions.reshape(-1, 1), used_col,
        jnp.where(row_used, positions, -1).reshape(entries, per_span),
        arrived.reshape(store_count * slot_depth, span_len, kv_width),
        (req_local, spans, per_span, span_len),
    )
    return (attended, new_kv)


def solution(mesh):
    placed = (
        P("store", "tensor"),
        P("tensor", "store"),
        P("store", None, "tensor"),
        P("store", "tensor"),
        P(),
        P(),
        P("store", None),
        P("store", None, None),
        P("store", None),
    )
    return jax.shard_map(
        body,
        mesh=mesh,
        in_specs=placed,
        out_specs=(P("store", "tensor"), P("store", "tensor")),
        check_vma=False,
    )
```

time: 682 us -> 365 us (0.54)
  waiting for transfers between devices: 464 us -> 0 us
  Pallas kernels: 0 us -> 348 us
  matrix products: 115 us -> 0 us
  local copies, waits for them, and re-layouts: 56.7 us -> 14.3 us
  other arithmetic: 23 us -> 2.19 us
  between operations: 14.1 us -> 0.71 us
  starting transfers between devices: 7.45 us -> 0 us
    pallas_call x0 -> x2, Pallas kernels: none -> 348 us  [the longest x1 306 us: exchange(): pl.pallas_call(functools.partial(exchange_kernel, n // 2, tensors), out_s...]
    all_gather x1 -> x0, waiting for transfers between devices: 327 us -> none  [body(): lax.all_gather(kv_weight, 'store', axis=1, tiled=True)]
    psum x1 -> x0, waiting for transfers between devices: 137 us -> none  [body(): summed = lax.psum(partial_kv, 'tensor')]
    dot_general x5 -> x0, matrix products: 60.4 us -> none  [the longest x2 33.7 us: blend_attend(): jnp.einsum('hgqk,khd->qhgd', weights, key_value[:, :, 1], preferred_eleme...]
    sub x2 -> x0, matrix products: 54.6 us -> none  [blend_attend(): raised = jnp.exp(scores - peak)]
    select_n x8 -> x1, other arithmetic: 13.3 us -> 0.67 us  [body(): jnp.where(row_used, positions, -1).reshape(entries, per_span)]
    dynamic_slice x8 -> x0, local copies, waits for them, and re-layouts: 12.6 us -> none  [body(): lax.map(one_request, (query_request, fresh_request, cached, span_order, p...]
    while x2 -> x0, local copies, waits for them, and re-layouts: 9.12 us -> none
  transfers between devices with their start and end apart: 3 -> 0, of which waited for: 2 -> 0; matrix products, arithmetic and copies ran while one was open for 7% -> 0% of each run, Pallas kernels for 0% -> 0%
where the time goes in v1:
time: 365 us
  Pallas kernels  348 us (95%)
  local copies, waits for them, and re-layouts  14.3 us (4%)
    pallas_call x1, Pallas kernels, exchange(): pl.pallas_call(functools.partial(exchange_kernel, n // 2, tensors), out_s...  306 us
    pallas_call x1, Pallas kernels, attend(): pl.pallas_call(functools.partial(attend_kernel, reqs, spans, per_span, sp...  41.7 us
    gather x1, local copies, waits for them, and re-layouts, body(): outgoing = jnp.take(pages, source_slot.reshape(-1), axis=0, mode='clip')  7.64 us

profile of v1, /device:TPU:0, one launch (start us, length us, event | category | flops | bytes accessed | tf_op | source)
XLA Modules:
  0.0 365.2 jit_solution(1410523036780146638)
XLA Ops:
  0.6 0.8 reshape.97
  1.4 0.3 convert_reduce_fusion
  1.7 0.1 add.29
  1.8 0.8 select_reduce_fusion.1
  2.7 0.1 broadcast_add_fusion
  2.7 0.7 add.32.span_sref
  3.4 0.6 reshape.98.page_sref
  4.0 0.8 mul.52
  4.8 0.2 select_reduce_fusion
  5.0 0.1 reshape.106
  5.1 0.0 copy-start.2
  5.1 7.6 %gather_fusion = bf16[64,128,512]{2,1,0:T(8,128)(2,1)} fusion(bf16[32,128,512]{2,1,0:T(8,128)(2,1)} %param.11, s32[1024]{0:T(1024)S(1)} %pad_clamp_fusion), kind=kCustom, calls=%fused_computation | custom fusion | bytes 16777472 | tf_op jit(solution)/shard_map/jit(_take)/gather | solution.py:406
  12.7 0.0 copy-done.2
  12.7 0.1 fusion.2
  12.8 1.3 reshape.113.used_ref.used_col
  14.1 0.0 copy-start.1
  14.1 306.3 %shard_map.104 = (bf16[1024,512]{1,0:T(8,128)(2,1)}, bf16[8,8,128,512]{3,2,1,0:T(8,128)(2,1)}) custom-call(bf16[1024,3072]{1,0:T(8,128)(2,1)} %hid_ref.1, bf16[3072,256]{1,0:T(8,128)(2,1)} %w_ref.1, bf16[8,8,128,512]{3,2,1,0:T(8,128)(2,1)} %bitcast.4, f32[1024,1]{1,0:T(8,128)} %reshape.113.used_ref.used_col), custom_call_target="tpu_custom_call" | custom-call | flops 12884901888 | bytes 40000000 | tf_op jit(solution)/shard_map/pallas_call | solution.py:237
  320.4 0.0 copy-done.1
  320.4 1.4 reshape.114.pos_col
  321.8 0.7 fusion.1
  322.5 0.0 copy-start
  322.5 41.7 %shard_map.105 = bf16[1024,1536]{1,0:T(8,128)(2,1)} custom-call(s32[32]{0:T(128)} %reshape.98.page_sref, s32[32]{0:T(128)} %add.32.span_sref, bf16[1024,1536]{1,0:T(8,128)(2,1)} %q_ref.1, bf16[1024,512]{1,0:T(8,128)(2,1)} %get-tuple-element.11.kv_ref, s32[1024,1]{1,0:T(8,128)} %reshape.114.pos_col, f32[1024,1]{1,0:T(8,128)} %reshape.113.used_ref.used_col, ...), custom_call_target="tpu_custom_call" | custom-call | tf_op jit(solution)/shard_map/pallas_call | solution.py:368
  364.2 0.0 copy-done
  364.2 1.0 copy.18
  (5 shorter events, 0.1 us)
Async XLA Ops:
  5.1 7.7 %copy-start.2 = (s32[2,16]{1,0:T(2,128)S(1)}, s32[2,16]{1,0:T(2,128)}, u32[]{:S(2)}) copy-start(s32[2,16]{1,0:T(2,128)} %param.17) | copy-start | bytes 388
  14.1 306.3 %copy-start.1 = (s32[2,16,32]{2,1,0:T(8,128)S(1)}, s32[2,16,32]{2,1,0:T(8,128)}, u32[]{:S(2)}) copy-start(s32[2,16,32]{2,1,0:T(8,128)} %param.16) | copy-start | bytes 12292
  322.5 41.7 %copy-start = (bf16[1024,512]{1,0:T(8,128)(2,1)S(1)}, bf16[1024,512]{1,0:T(8,128)(2,1)}, u32[]{:S(2)}) copy-start(bf16[1024,512]{1,0:T(8,128)(2,1)} %get-tuple-element.11.kv_ref) | copy-start | bytes 3145732

commit v2 on v1

--- a/solution.py
+++ b/solution.py
@@ -14,8 +14,8 @@
 
 
 def exchange_kernel(
-    line, tensors, hid_ref, w_ref, out_ref, used_ref, kv_ref, arr_ref,
-    wbuf, own, sendbuf, recvbuf,
+    line, tensors, pick_ref, hid_ref, w_ref, page_ref, used_ref, kv_ref, arr_ref,
+    out_ref, wbuf, own, sendbuf, recvbuf,
     loc_sem, up_sem, dn_sem, x_sem, wrecv, psend, precv, rsend, rrecv,
 ):
     me = lax.axis_index("store")
@@ -36,8 +36,6 @@
         )
     own_w = pltpu.make_async_copy(w_ref, wbuf.at[me], loc_sem.at[0])
     own_w.start()
-    own_pages = pltpu.make_async_copy(out_ref.at[me], arr_ref.at[me], loc_sem.at[1])
-    own_pages.start()
     own_w.wait()
     pl.semaphore_wait(barrier, n - 1 + tensors - 1)
 
@@ -110,6 +108,15 @@
         down(me).start()
 
     across(me).start()
+    depth = out_ref.shape[1]
+
+    def choose(i, carry):
+        out_ref[i // depth, i % depth] = page_ref[pick_ref[i]]
+        return carry
+
+    lax.fori_loop(0, n * depth, choose, 0)
+    own_pages = pltpu.make_async_copy(out_ref.at[me], arr_ref.at[me], loc_sem.at[1])
+    own_pages.start()
     compute(me)
 
     def hop(k, carry):
@@ -137,21 +144,19 @@
 
             across(slot).start()
 
-        @pl.when(k == 1)
-        def _():
-            def same(i, c):
-                page_copy(((a + i) % line) * 2 + b).start()
+        @pl.when(k == 2)
+        def _():
+            def launch(i, c):
+                place = jnp.where(2 * a >= line, i, line - 1 - i)
+
+                @pl.when(place != a)
+                def _():
+                    page_copy(place * 2 + b).start()
+
+                page_copy(place * 2 + 1 - b).start()
                 return c
 
-            lax.fori_loop(1, line, same, 0)
-
-        @pl.when(k == line - 1)
-        def _():
-            def other(i, c):
-                page_copy(((a + i) % line) * 2 + 1 - b).start()
-                return c
-
-            lax.fori_loop(0, line, other, 0)
+            lax.fori_loop(0, line, launch, 0)
 
         for place in (low, high):
             @pl.when((place >= 0) & (place < line))
@@ -229,7 +234,7 @@
     own_pages.wait()
 
 
-def exchange(hidden, kv_weight, outgoing, used, n, tensors):
+def exchange(picks, hidden, kv_weight, pages, depth_slots, used, n, tensors):
     rows, depth = hidden.shape
     width = kv_weight.shape[1]
     per_owner = n // tensors
@@ -238,12 +243,13 @@
         functools.partial(exchange_kernel, n // 2, tensors),
         out_shape=(
             jax.ShapeDtypeStruct((rows, per_owner * width), jnp.bfloat16),
-            jax.ShapeDtypeStruct(outgoing.shape, outgoing.dtype),
+            jax.ShapeDtypeStruct((n, depth_slots) + pages.shape[1:], pages.dtype),
         ),
         in_specs=[
+            pl.BlockSpec(memory_space=pltpu.SMEM),
             pl.BlockSpec(memory_space=pltpu.VMEM),
             pl.BlockSpec(memory_space=pl.ANY),
-            pl.BlockSpec(memory_space=pl.ANY),
+            pl.BlockSpec(memory_space=pltpu.VMEM),
             pl.BlockSpec(memory_space=pltpu.VMEM),
         ],
         out_specs=(
@@ -251,6 +257,7 @@
             pl.BlockSpec(memory_space=pl.ANY),
         ),
         scratch_shapes=[
+            pltpu.VMEM((n, depth_slots) + pages.shape[1:], pages.dtype),
             pltpu.VMEM((n, depth, width), jnp.bfloat16),
             pltpu.VMEM((per_owner, rows, width), jnp.float32),
             pltpu.VMEM((n, rows, width), jnp.bfloat16),
@@ -264,7 +271,7 @@
         cost_estimate=pl.CostEstimate(
             flops=2 * rows * depth * n * width, bytes_accessed=4 * 10**7, transcendentals=0
         ),
-    )(hidden, kv_weight, outgoing, used)
+    )(picks, hidden, kv_weight, pages, used)
 
 
 GROUP = 4
@@ -302,7 +309,7 @@
         return c
 
     lax.fori_loop(0, reqs * spans, blend, 0)
-    scale = HEAD ** (-0.5)
+    scale = HEAD ** (-0.5) * 1.4426950408889634
     block = fold * per_span
 
     def one(i, carry):
@@ -313,38 +320,52 @@
                 length = (g + 1) * GROUP * span_len
                 free = g * GROUP * span_len
                 base = pl.multiple_of(r * spans * span_len, span_len)
+                for ii in range(GROUP):
+                    span = span_sref[r * spans + g * GROUP + ii]
+                    rows = pl.ds(pl.multiple_of(span * per_span, per_span), per_span)
+                    limit = pos_col[rows, :]
+                    for m in range(fold):
+                        at = ii * block + m * per_span
+                        lim[at : at + per_span, :] = limit
+                        for h in range(heads):
+                            col = (h * fold + m) * HEAD
+                            qbuf[h, at : at + per_span, :] = q_ref[rows, col : col + HEAD]
+                for h in range(heads):
+                    key = keys[pl.ds(base, length), 2 * h * HEAD : (2 * h + 1) * HEAD]
+                    sbuf[h, :, :length] = lax.dot_general(
+                        qbuf[h], key, (((1,), (1,)), ((), ())),
+                        preferred_element_type=jnp.float32,
+                    )
                 for h in range(heads):
                     for ii in range(GROUP):
-                        span = span_sref[r * spans + g * GROUP + ii]
-                        rows = pl.ds(pl.multiple_of(span * per_span, per_span), per_span)
-                        limit = pos_col[rows, :] + ii * span_len
-                        for m in range(fold):
-                            col = (h * fold + m) * HEAD
-                            at = ii * block + m * per_span
-                            qbuf[at : at + per_span, :] = q_ref[rows, col : col + HEAD]
-                            if h == 0:
-                                lim[at : at + per_span, :] = limit
-                    key = keys[pl.ds(base, length), 2 * h * HEAD : (2 * h + 1) * HEAD]
-                    val = keys[pl.ds(base, length), (2 * h + 1) * HEAD : (2 * h + 2) * HEAD]
-                    sbuf[:, :length] = lax.dot_general(
-                        qbuf[...], key, (((1,), (1,)), ((), ())),
-                        preferred_element_type=jnp.float32,
-                    )
-                    for ii in range(GROUP):
                         sl = slice(ii * block, (ii + 1) * block)
-                        tail = sbuf[sl, free:length]
-                        place = lax.broadcasted_iota(jnp.int32, tail.shape, 1)
-                        tail = jnp.where(place <= lim[sl, :], tail, -1e30)
-                        if g:
-                            score = jnp.concatenate([sbuf[sl, :free], tail], axis=1)
-                        else:
-                            score = tail
-                        peak = jnp.max(score, axis=1, keepdims=True)
-                        raised = jnp.exp((score - peak) * scale)
+                        open_to = free + ii * span_len
+                        last = sbuf[h, sl, open_to : open_to + span_len]
+                        place = lax.broadcasted_iota(jnp.int32, last.shape, 1)
+                        last = jnp.where(place <= lim[sl, :], last, -1e30)
+                        peak = jnp.max(last, axis=1, keepdims=True)
+                        if open_to:
+                            peak = jnp.maximum(
+                                peak, jnp.max(sbuf[h, sl, :open_to], axis=1, keepdims=True)
+                            )
+                        peak = peak * scale
+                        raised = jnp.exp2(last * scale - peak)
                         total = jnp.sum(raised, axis=1, keepdims=True)
+                        vcol = slice((2 * h + 1) * HEAD, (2 * h + 2) * HEAD)
                         mixed = jnp.dot(
-                            raised.astype(jnp.bfloat16), val, preferred_element_type=jnp.float32
-                        ) / total
+                            raised.astype(jnp.bfloat16),
+                            keys[pl.ds(base + open_to, span_len), vcol],
+                            preferred_element_type=jnp.float32,
+                        )
+                        if open_to:
+                            raised = jnp.exp2(sbuf[h, sl, :open_to] * scale - peak)
+                            total += jnp.sum(raised, axis=1, keepdims=True)
+                            mixed += jnp.dot(
+                                raised.astype(jnp.bfloat16),
+                                keys[pl.ds(base, open_to), vcol],
+                                preferred_element_type=jnp.float32,
+                            )
+                        mixed = mixed / total
                         span = span_sref[r * spans + g * GROUP + ii]
                         rows = pl.ds(pl.multiple_of(span * per_span, per_span), per_span)
                         used = used_col[rows, :]
@@ -373,8 +394,8 @@
         scratch_shapes=[
             pltpu.VMEM((total, span_len, new_kv.shape[1]), jnp.bfloat16),
             pltpu.VMEM((total * span_len, new_kv.shape[1]), jnp.bfloat16),
-            pltpu.VMEM((GROUP * fold * per_span, HEAD), jnp.bfloat16),
-            pltpu.VMEM((GROUP * fold * per_span, spans * span_len), jnp.float32),
+            pltpu.VMEM((heads, GROUP * fold * per_span, HEAD), jnp.bfloat16),
+            pltpu.VMEM((heads, GROUP * fold * per_span, spans * span_len), jnp.float32),
             pltpu.VMEM((GROUP * fold * per_span, 1), jnp.int32),
             pltpu.SemaphoreType.DMA((total,)),
         ],
@@ -403,10 +424,11 @@
         owner_rank[:, :, None] == jnp.arange(slot_depth)[None, None, :]
     )
     source_slot = jnp.sum(picked * slot_table[:, :, None], axis=1)
-    outgoing = jnp.take(pages, source_slot.reshape(-1), axis=0, mode="clip")
-    outgoing = outgoing.reshape(store_count, slot_depth, span_len, kv_width)
-    if kv_weight.shape[1] % 128 == 0 and store_count % tensors == 0:
-        new_kv, arrived = exchange(hidden, kv_weight, outgoing, used_col, store_count, tensors)
+    picks = source_slot.reshape(-1).astype(jnp.int32)
+    if kv_weight.shape[1] % 128 == 0 and store_count % tensors == 0 and store_count >= 6:
+        new_kv, arrived = exchange(
+            picks, hidden, kv_weight, pages, slot_depth, used_col, store_count, tensors
+        )
     else:
         partial_kv = jnp.dot(
             hidden,
@@ -415,6 +437,9 @@
         )
         own_kv = lax.psum_scatter(partial_kv, "tensor", scatter_dimension=1, tiled=True)
         new_kv = (own_kv * used_col).astype(jnp.bfloat16)
+        outgoing = jnp.take(pages, picks, axis=0, mode="clip").reshape(
+            store_count, slot_depth, span_len, kv_width
+        )
         arrived = lax.all_to_all(outgoing, "store", split_axis=0, concat_axis=0, tiled=True)
     my_owner = lax.dynamic_index_in_dim(owners, store_index, 0, keepdims=False)
     my_rank = lax.dynamic_index_in_dim(owner_rank, store_index, 0, keepdims=False)

time: 365 us -> 323 us (0.88)
  Pallas kernels: 348 us -> 311 us
  local copies, waits for them, and re-layouts: 14.3 us -> 7.85 us
    pallas_call x1, Pallas kernels: 306 us -> 274 us  [exchange(): pl.pallas_call(functools.partial(exchange_kernel, n // 2, tensors), out_s...]
    gather x1 -> x0, local copies, waits for them, and re-layouts: 7.64 us -> none  [body(): outgoing = jnp.take(pages, source_slot.reshape(-1), axis=0, mode='clip')]
    pallas_call x1, Pallas kernels: 41.7 us -> 36.8 us  [attend(): pl.pallas_call(functools.partial(attend_kernel, reqs, spans, per_span, sp...]
where the time goes in v2:
time: 323 us
  Pallas kernels  311 us (96%)
  local copies, waits for them, and re-layouts  7.85 us (2%)
  other arithmetic  3.58 us (1%)
    pallas_call x1, Pallas kernels, exchange(): pl.pallas_call(functools.partial(exchange_kernel, n // 2, tensors), out_s...  274 us
    pallas_call x1, Pallas kernels, attend(): pl.pallas_call(functools.partial(attend_kernel, reqs, spans, per_span, sp...  36.8 us

profile of v2, /device:TPU:0, one launch (start us, length us, event | category | flops | bytes accessed | tf_op | source)
XLA Modules:
  0.0 322.7 jit_solution(755773146600656639)
XLA Ops:
  0.6 0.8 reshape.95
  1.4 0.8 mul.52
  2.2 0.3 convert_reduce_fusion
  2.5 0.2 select_reduce_fusion
  2.7 0.6 reshape.97.pick_ref
  3.3 0.1 add.29
  3.4 0.8 select_reduce_fusion.1
  4.2 0.1 broadcast_add_fusion
  4.3 0.7 add.32.span_sref
  5.0 0.6 reshape.96.page_sref
  5.6 1.4 fusion.1
  7.0 0.7 fusion.2
  7.7 1.3 reshape.102.used_ref.used_col
  9.1 2.0 reshape.103.pos_col
  11.1 273.9 %shard_map.104 = (bf16[1024,512]{1,0:T(8,128)(2,1)}, bf16[8,8,128,512]{3,2,1,0:T(8,128)(2,1)}) custom-call(s32[64]{0:T(128)} %reshape.97.pick_ref, bf16[1024,3072]{1,0:T(8,128)(2,1)} %hid_ref.1, bf16[3072,256]{1,0:T(8,128)(2,1)} %w_ref.1, bf16[32,128,512]{2,1,0:T(8,128)(2,1)} %page_ref.1, f32[1024,1]{1,0:T(8,128)} %reshape.102.used_ref.used_col), custom_call_target="tpu_custom_call" | custom-call | flops 12884901888 | bytes 40000000 | tf_op jit(solution)/shard_map/pallas_call | solution.py:242
  285.0 0.0 copy-start
  285.0 36.8 %shard_map.105 = bf16[1024,1536]{1,0:T(8,128)(2,1)} custom-call(s32[32]{0:T(128)} %reshape.96.page_sref, s32[32]{0:T(128)} %add.32.span_sref, bf16[1024,1536]{1,0:T(8,128)(2,1)} %q_ref.1, bf16[1024,512]{1,0:T(8,128)(2,1)} %get-tuple-element.11.kv_ref, s32[1024,1]{1,0:T(8,128)} %reshape.103.pos_col, f32[1024,1]{1,0:T(8,128)} %reshape.102.used_ref.used_col, ...), custom_call_target="tpu_custom_call" | custom-call | tf_op jit(solution)/shard_map/pallas_call | solution.py:389
  321.8 0.0 copy-done
  321.8 1.0 copy.18
  (4 shorter events, 0.0 us)
Async XLA Ops:
  285.0 36.8 %copy-start = (bf16[1024,512]{1,0:T(8,128)(2,1)S(1)}, bf16[1024,512]{1,0:T(8,128)(2,1)}, u32[]{:S(2)}) copy-start(bf16[1024,512]{1,0:T(8,128)(2,1)} %get-tuple-element.11.kv_ref) | copy-start | bytes 3145732

commit v3 on v2

--- a/solution.py
+++ b/solution.py
@@ -9,6 +9,16 @@
 
 HEAD = 128
 MESH_ID = pl.DeviceIdType.MESH
+
+
+def as_column(row):
+    count = row.shape[1]
+    eye = lax.broadcasted_iota(jnp.int32, (count, count), 0) == lax.broadcasted_iota(
+        jnp.int32, (count, count), 1
+    )
+    return jnp.sum(jnp.where(eye, row, 0.0), axis=1, keepdims=True)
+
+
 ROW_TILE = 256
 VMEM_BYTES = 60 * 1024 * 1024
 
@@ -193,18 +203,19 @@
 
     lax.fori_loop(1, tensors, collect, 0)
 
+    groups, per_group = used_ref.shape
+
     def finish(i, carry):
-        rows = pl.ds(pl.multiple_of(i * ROW_TILE, ROW_TILE), ROW_TILE)
+        rows = pl.ds(pl.multiple_of(i * per_group, per_group), per_group)
+        keep = as_column(used_ref[pl.ds(i, 1), :])
         for q in range(per_owner):
             total = own[q, rows, :]
             for j in range(1, tensors):
                 total += recvbuf[(tm + j) % tensors, q, rows, :].astype(jnp.float32)
-            kv_ref[rows, q * width : (q + 1) * width] = (total * used_ref[rows, :]).astype(
-                kv_ref.dtype
-            )
-        return carry
-
-    lax.fori_loop(0, hid_ref.shape[0] // ROW_TILE, finish, 0)
+            kv_ref[rows, q * width : (q + 1) * width] = (total * keep).astype(kv_ref.dtype)
+        return carry
+
+    lax.fori_loop(0, groups, finish, 0)
 
     def drain(slot, carry):
         @pl.when(slot // per_owner != tm)
@@ -279,7 +290,7 @@
 
 def attend_kernel(
     reqs, spans, per_span, span_len, heads, fold,
-    page_sref, span_sref, q_ref, kv_ref, pos_col, used_col, pos_row, arr_ref, out_ref,
+    page_sref, span_sref, q_ref, kv_ref, pos_row, arr_ref, out_ref,
     page, keys, qbuf, sbuf, lim, page_sem,
 ):
     def fetch(i):
@@ -291,24 +302,31 @@
 
     lax.fori_loop(0, reqs * spans, start, 0)
 
-    def blend(i, c):
+    def blend_one(i):
         fetch(i).wait()
         span = span_sref[i]
         marks = pos_row[pl.ds(span, 1), :]
         hit = lax.broadcasted_iota(jnp.int32, (span_len, per_span), 0) == marks
+        hit = hit.astype(jnp.float32)
         fresh = kv_ref[pl.ds(pl.multiple_of(span * per_span, per_span), per_span), :]
-        placed = jnp.dot(
-            hit.astype(jnp.float32).astype(jnp.bfloat16), fresh,
-            preferred_element_type=jnp.float32,
-        )
-        replaced = jnp.max(hit.astype(jnp.float32), axis=1, keepdims=True) > 0.5
-        mixed = jnp.where(replaced, placed, page[i].astype(jnp.float32))
+        kept = 1.0 - jnp.max(hit, axis=1, keepdims=True)
+        eye = lax.broadcasted_iota(jnp.int32, (span_len, span_len), 0) == (
+            lax.broadcasted_iota(jnp.int32, (span_len, span_len), 1)
+        )
+        kept = jnp.where(eye, kept, 0.0)
+        mixed = jnp.dot(
+            hit.astype(jnp.bfloat16), fresh, preferred_element_type=jnp.float32
+        ) + jnp.dot(kept.astype(jnp.bfloat16), page[i], preferred_element_type=jnp.float32)
         keys[pl.ds(pl.multiple_of(i * span_len, span_len), span_len), :] = mixed.astype(
             jnp.bfloat16
         )
+
+    def blend(i, c):
+        for step in range(GROUP):
+            blend_one(i * GROUP + step)
         return c
 
-    lax.fori_loop(0, reqs * spans, blend, 0)
+    lax.fori_loop(0, reqs * spans // GROUP, blend, 0)
     scale = HEAD ** (-0.5) * 1.4426950408889634
     block = fold * per_span
 
@@ -320,10 +338,13 @@
                 length = (g + 1) * GROUP * span_len
                 free = g * GROUP * span_len
                 base = pl.multiple_of(r * spans * span_len, span_len)
+                useds = []
                 for ii in range(GROUP):
                     span = span_sref[r * spans + g * GROUP + ii]
                     rows = pl.ds(pl.multiple_of(span * per_span, per_span), per_span)
-                    limit = pos_col[rows, :]
+                    limit = as_column(pos_row[pl.ds(span, 1), :].astype(jnp.float32))
+                    useds.append((limit >= 0.0).astype(jnp.float32))
+                    limit = limit.astype(jnp.int32)
                     for m in range(fold):
                         at = ii * block + m * per_span
                         lim[at : at + per_span, :] = limit
@@ -368,7 +389,7 @@
                         mixed = mixed / total
                         span = span_sref[r * spans + g * GROUP + ii]
                         rows = pl.ds(pl.multiple_of(span * per_span, per_span), per_span)
-                        used = used_col[rows, :]
+                        used = useds[ii]
                         for m in range(fold):
                             col = (h * fold + m) * HEAD
                             out_ref[rows, col : col + HEAD] = (
@@ -379,7 +400,7 @@
     lax.fori_loop(0, reqs * (spans // GROUP), one, 0)
 
 
-def attend(page_at, span_at, queries, new_kv, pos_col, used_col, pos_row, arrived, shape):
+def attend(page_at, span_at, queries, new_kv, pos_row, arrived, shape):
     reqs, spans, per_span, span_len = shape
     heads = new_kv.shape[1] // (2 * HEAD)
     fold = queries.shape[1] // (heads * HEAD)
@@ -389,7 +410,7 @@
     return pl.pallas_call(
         functools.partial(attend_kernel, reqs, spans, per_span, span_len, heads, fold),
         out_shape=jax.ShapeDtypeStruct(queries.shape, queries.dtype),
-        in_specs=[sm, sm, vm, vm, vm, vm, vm, pl.BlockSpec(memory_space=pl.ANY)],
+        in_specs=[sm, sm, vm, vm, vm, pl.BlockSpec(memory_space=pl.ANY)],
         out_specs=vm,
         scratch_shapes=[
             pltpu.VMEM((total, span_len, new_kv.shape[1]), jnp.bfloat16),
@@ -400,7 +421,7 @@
             pltpu.SemaphoreType.DMA((total,)),
         ],
         compiler_params=pltpu.CompilerParams(vmem_limit_bytes=VMEM_BYTES),
-    )(page_at, span_at, queries, new_kv, pos_col, used_col, pos_row, arrived)
+    )(page_at, span_at, queries, new_kv, pos_row, arrived)
 
 
 def body(hidden, kv_weight, pages, queries, page_owner, page_slot, span_order, positions, counts):
@@ -414,7 +435,7 @@
     span_len = pages.shape[1]
     kv_width = pages.shape[2]
     row_used = jnp.arange(per_span)[None, None, :] < counts[:, :, None]
-    used_col = row_used.reshape(-1, 1).astype(jnp.float32)
+    used_row = row_used.reshape(entries, per_span).astype(jnp.float32)
     owners = page_owner.reshape(store_count, entries)
     slot_table = page_slot.reshape(store_count, entries)
     before = jnp.arange(entries)[None, :] < jnp.arange(entries)[:, None]
@@ -427,7 +448,7 @@
     picks = source_slot.reshape(-1).astype(jnp.int32)
     if kv_weight.shape[1] % 128 == 0 and store_count % tensors == 0 and store_count >= 6:
         new_kv, arrived = exchange(
-            picks, hidden, kv_weight, pages, slot_depth, used_col, store_count, tensors
+            picks, hidden, kv_weight, pages, slot_depth, used_row, store_count, tensors
         )
     else:
         partial_kv = jnp.dot(
@@ -436,7 +457,7 @@
             preferred_element_type=jnp.float32,
         )
         own_kv = lax.psum_scatter(partial_kv, "tensor", scatter_dimension=1, tiled=True)
-        new_kv = (own_kv * used_col).astype(jnp.bfloat16)
+        new_kv = (own_kv * used_row.reshape(-1, 1)).astype(jnp.bfloat16)
         outgoing = jnp.take(pages, picks, axis=0, mode="clip").reshape(
             store_count, slot_depth, span_len, kv_width
         )
@@ -450,7 +471,6 @@
     span_at = (span_at + jnp.arange(req_local)[:, None] * spans).reshape(-1)
     attended = attend(
         page_at.reshape(-1).astype(jnp.int32), span_at.astype(jnp.int32), queries, new_kv,
-        positions.reshape(-1, 1), used_col,
         jnp.where(row_used, positions, -1).reshape(entries, per_span),
         arrived.reshape(store_count * slot_depth, span_len, kv_width),
         (req_local, spans, per_span, span_len),

time: 323 us -> 327 us (1.012)
  Pallas kernels: 311 us -> 315 us
    pallas_call x1, Pallas kernels: 36.8 us -> 40.8 us  [attend(): pl.pallas_call(functools.partial(attend_kernel, reqs, spans, per_span, sp...]
where the time goes in v3:
time: 327 us; the launch traced here: 324 us
  Pallas kernels  315 us (96%)
  local copies, waits for them, and re-layouts  5.28 us (2%)
  other arithmetic  3.51 us (1%)
    pallas_call x1, Pallas kernels, exchange(): pl.pallas_call(functools.partial(exchange_kernel, n // 2, tensors), out_s...  274 us
    pallas_call x1, Pallas kernels, attend(): pl.pallas_call(functools.partial(attend_kernel, reqs, spans, per_span, sp...  40.8 us

profile of v3, /device:TPU:0, one launch (start us, length us, event | category | flops | bytes accessed | tf_op | source)
XLA Modules:
  0.0 324.1 jit_solution(17138471224985456149)
XLA Ops:
  0.6 0.8 lt.49
  1.4 0.8 reshape.67
  2.2 0.8 mul.52
  2.9 0.3 convert_reduce_fusion
  3.3 0.2 select_reduce_fusion
  3.5 0.6 reshape.69.pick_ref
  4.1 0.1 add.29
  4.2 0.8 select_reduce_fusion.1
  5.0 0.1 broadcast_add_fusion
  5.1 0.7 add.32.span_sref
  5.7 0.7 reshape.68.page_sref
  6.4 0.7 fusion.1.used_ref
  7.1 1.4 fusion.2
  8.5 273.8 %shard_map.104 = (bf16[1024,512]{1,0:T(8,128)(2,1)}, bf16[8,8,128,512]{3,2,1,0:T(8,128)(2,1)}) custom-call(s32[64]{0:T(128)} %reshape.69.pick_ref, bf16[1024,3072]{1,0:T(8,128)(2,1)} %hid_ref.1, bf16[3072,256]{1,0:T(8,128)(2,1)} %w_ref.1, bf16[32,128,512]{2,1,0:T(8,128)(2,1)} %page_ref.1, f32[32,32]{1,0:T(8,128)} %fusion.1.used_ref), custom_call_target="tpu_custom_call" | custom-call | flops 12884901888 | bytes 40000000 | tf_op jit(solution)/shard_map/pallas_call | solution.py:253
  282.3 0.0 copy-start
  282.3 40.8 %shard_map.105 = bf16[1024,1536]{1,0:T(8,128)(2,1)} custom-call(s32[32]{0:T(128)} %reshape.68.page_sref, s32[32]{0:T(128)} %add.32.span_sref, bf16[1024,1536]{1,0:T(8,128)(2,1)} %q_ref.1, bf16[1024,512]{1,0:T(8,128)(2,1)} %get-tuple-element.11.kv_ref, s32[32,32]{1,0:T(8,128)} %bitcast.3, bf16[64,128,512]{2,1,0:T(8,128)(2,1)} %bitcast.2), custom_call_target="tpu_custom_call" | custom-call | tf_op jit(solution)/shard_map/pallas_call | solution.py:410
  323.2 0.0 copy-done
  323.2 1.0 copy.12
  (4 shorter events, 0.0 us)
Async XLA Ops:
  282.3 40.9 %copy-start = (bf16[1024,512]{1,0:T(8,128)(2,1)S(1)}, bf16[1024,512]{1,0:T(8,128)(2,1)}, u32[]{:S(2)}) copy-start(bf16[1024,512]{1,0:T(8,128)(2,1)} %get-tuple-element.11.kv_ref) | copy-start | bytes 3145732
